TPU v7x, 256 devices: a whole 4x4x8 slice. The times are simulated.
256 devices in a mesh: ctx: 16 (over x, z_lo), tp: 16 (over y, z_hi, core).
Axes of the slice: x: 4, y: 4, z: 8 (z_hi: 2, z_lo: 4; z = z_hi * 4 + z_lo), core: 2. Of those that a mesh axis runs over, the one named last changes fastest.
Arguments:
- layer_input: bfloat16 [4096, 7168], P('ctx', 'tp'), may hold values from -6 to 6
- q_latent: bfloat16 [4096, 1536], P('ctx'), may hold values from -384 to 384
- w_dkv: bfloat16 [7168, 576], P('tp'), may hold values from -0.0625 to 0.0625
- kv_gain: float32 [512], replicated, may hold values from 0.1 to 1.9
- w_uq: bfloat16 [1536, 12288], P(None, 'tp'), may hold values from -0.15625 to 0.15625
- w_uk: bfloat16 [64, 512, 128], P('tp'), may hold values from -1 to 1
- w_uv: bfloat16 [64, 512, 128], P('tp'), may hold values from -0.25 to 0.25
- w_o: bfloat16 [8192, 7168], P('tp'), may hold values from -0.09375 to 0.09375
- block_order: int32 [32], replicated, may hold values from 0 to 31, each once
- owner_slot: int32 [32], replicated, may hold values from 0 to 31, each once
Outputs:
- layer_out: bfloat16 [4096, 7168], P('ctx', 'tp')
- owner_cache: bfloat16 [4096, 576], P('ctx')
Inputs may be any that keep to these rules, and one draw needn't show every extreme that they name: `block_order`: each of 0 to 31 once. `owner_slot`: each of 0 to 31 once.
All inputs are finite; a program needn't handle non-finite values.
Results may differ from a plain program's by a relative error of at most 0.02.
The roundings to bfloat16 on the way count: a program that leaves them out, or rounds other values in their place, can miss the bound.
Values may be sent and summed in bfloat16 or wider, within the bound.
A program may use at most 128 MiB of HBM per device.

v0:
```python
import math

import jax
import jax.numpy as jnp
from jax import lax
from jax.sharding import PartitionSpec as P


def rotate(values_in, places):
    width = values_in.shape[-1]
    half_w = width // 2
    frequency = jnp.exp(jnp.arange(half_w).astype(jnp.float32) * (-2.0 * math.log(10000.0) / width))
    angles = places.astype(jnp.float32)[:, None] * frequency[None, :]
    cosine = jnp.cos(angles)
    sines = jnp.sin(angles)
    front_part = values_in[..., :half_w]
    back_part = values_in[..., half_w:]
    return jnp.concatenate(
        [front_part * cosine - back_part * sines, front_part * sines + back_part * cosine], -1
    )


def finish_rows(kv_rows, places, kv_gain, latent):
    compressed = kv_rows[:, :latent]
    mean_square = jnp.mean(compressed * compressed, axis=1, keepdims=True)
    compressed = compressed * lax.rsqrt(mean_square + 1e-06) * kv_gain
    return jnp.concatenate([compressed, rotate(kv_rows[:, latent:], places)], 1).astype(
        jnp.bfloat16
    )


def block_starts(global_rows, block_order, half_rows):
    blocks = block_order.shape[0]
    matches = (global_rows // half_rows)[:, None] == jnp.arange(blocks, dtype=jnp.int32)[None, :]
    chosen = jnp.sum(jnp.where(matches, block_order[None, :], 0), axis=1)
    return chosen * half_rows + global_rows % half_rows


def lookup_inverse(lookup, wanted):
    matches = wanted[:, None] == lookup[None, :]
    return jnp.sum(
        jnp.where(matches, jnp.arange(lookup.shape[0], dtype=jnp.int32)[None, :], 0), axis=1
    )


def per_device(
    layer_input, q_latent, w_dkv, kv_gain, w_uq, w_uk, w_uv, w_o, block_order, owner_slot
):
    tok_rows = q_latent.shape[0]
    half_rows = tok_rows // 2
    head_count = w_uk.shape[0]
    latent = w_uk.shape[1]
    nope_width = w_uk.shape[2]
    qk_width = w_uq.shape[1] // head_count
    score_scale = qk_width ** (-0.5)
    ctx_place = lax.axis_index("ctx")
    local_rows = jnp.arange(tok_rows, dtype=jnp.int32)
    own_rows = ctx_place * tok_rows + local_rows
    query_places = block_starts(own_rows, block_order, half_rows)
    q_proj = jnp.dot(q_latent, w_uq, preferred_element_type=jnp.float32)
    q_proj = q_proj.reshape(tok_rows, head_count, qk_width).transpose(1, 0, 2)
    q_nope = q_proj[..., :nope_width].astype(jnp.bfloat16)
    q_absorbed = jnp.einsum(
        "hqn,hln->hql", q_nope, w_uk, preferred_element_type=jnp.float32
    ).astype(jnp.bfloat16)
    q_rotary = rotate(q_proj[..., nope_width:], query_places).astype(jnp.bfloat16)
    queries = jnp.concatenate([q_absorbed, q_rotary], axis=2)
    slot_index = 2 * ctx_place + local_rows // half_rows
    prompt_block = lookup_inverse(owner_slot, slot_index)
    held_block = lookup_inverse(block_order, prompt_block)
    source_rows = held_block * half_rows + local_rows % half_rows
    partial_value = jnp.dot(layer_input, w_dkv, preferred_element_type=jnp.float32)
    kv_full = lax.psum(partial_value, "tp")
    own_cache = finish_rows(kv_full, query_places, kv_gain, latent)
    kv_piece = lax.all_gather(own_cache, "ctx", axis=0, tiled=True)
    m_run = jnp.full((head_count, tok_rows), -1e30, jnp.float32)
    piece_rows = kv_piece.shape[0]
    key_rows = jnp.arange(piece_rows, dtype=jnp.int32)
    key_places = block_starts(key_rows, block_order, half_rows)
    visible = key_places[None, :] <= query_places[:, None]
    scores = (
        jnp.einsum("hqc,kc->hqk", queries, kv_piece, preferred_element_type=jnp.float32)
        * score_scale
    )
    scores = jnp.where(visible[None], scores, -1e30)
    m_new = jnp.maximum(m_run, jnp.max(scores, axis=2))
    weights = jnp.where(visible[None], jnp.exp(scores - m_new[..., None]), 0.0)
    l_new = jnp.sum(weights, axis=2)
    acc_new = jnp.einsum(
        "hqk,kl->hql",
        weights.astype(jnp.bfloat16),
        kv_piece[:, :latent],
        preferred_element_type=jnp.float32,
    )
    picked = (source_rows[:, None] == key_rows[None, :]).astype(jnp.bfloat16)
    cache_run = jnp.dot(picked, kv_piece, preferred_element_type=jnp.float32)
    folded = (m_new, l_new, acc_new, cache_run)
    m_fin, l_fin, acc_fin, cache_fin = folded
    context = (acc_fin / l_fin[..., None]).astype(jnp.bfloat16)
    head_values = jnp.einsum(
        "hql,hlv->qhv", context, w_uv, preferred_element_type=jnp.float32
    ).astype(jnp.bfloat16)
    head_values = head_values.reshape(tok_rows, head_count * w_uv.shape[2])
    out_share = lax.psum_scatter(
        jnp.einsum("fc,tf->ct", w_o, head_values, preferred_element_type=jnp.float32).astype(
            jnp.bfloat16
        ),
        "tp",
        scatter_dimension=0,
        tiled=True,
    ).astype(jnp.float32)
    return (out_share.T.astype(jnp.bfloat16), cache_fin.astype(jnp.bfloat16))


def solution(mesh):
    return jax.shard_map(
        per_device,
        mesh=mesh,
        in_specs=(
            P("ctx", "tp"),
            P("ctx", None),
            P("tp", None),
            P(),
            P(None, "tp"),
            P("tp", None, None),
            P("tp", None, None),
            P("tp", None),
            P(),
            P(),
        ),
        out_specs=(P("ctx", "tp"), P("ctx", None)),
        check_vma=False,
    )
```

profile of v0, /device:TPU:1, one launch (start us, length us, event | category | flops | bytes accessed | tf_op | source)
XLA Modules:
  0.0 463.9 jit_solution(5419131475492307525)
XLA Ops:
  7.2 2.5 fusion.45
  9.9 0.7 select_reduce_fusion.2
  10.6 0.7 select_reduce_fusion.1
  11.4 177.9 %all-reduce.2.cloned.1.call-done = f32[256,576]{0,1:T(8,128)} async-done(((f32[256,576]{0,1:T(8,128)}), f32[256,576]{0,1:T(8,128)}) %all-reduce.2.cloned.1.call-update) | async-done | bytes 589840 | tf_op jit(solution)/shard_map/psum | solution.py:73
  189.3 1.1 multiply_reduce_fusion
  190.4 1.6 multiply_cosine_fusion
  192.0 1.2 multiply_convert_fusion
  193.2 0.7 pad_maximum_fusion
  194.0 3.0 fusion.44
  197.0 1.5 copy.27
  198.7 2.5 convolution_convert_fusion.1
  201.2 1.7 broadcast_compare_fusion
  202.8 0.9 copy.28
  203.7 1.5 copy.29
  205.2 1.9 subtract_convert_fusion
  207.2 103.4 %all-gather.2.cloned.1.call-done = bf16[4096,576]{0,1:T(8,128)(2,1)} async-done(((bf16[256,576]{0,1:T(8,128)(2,1)}), bf16[4096,576]{0,1:T(8,128)(2,1)}) %all-gather.2.cloned.1.call-update) | async-done | bytes 4718608 | tf_op jit(solution)/shard_map/all_gather | solution.py:75
  310.5 10.5 %fusion = (f32[4,256]{1,0:T(4,128)S(1)}, f32[4,256,4096]{2,1,0:T(8,128)S(1)}) fusion(pred[256,4096]{1,0:T(8,128)(4,1)} %broadcast_compare_fusion, bf16[4096,576]{0,1:T(8,128)(2,1)} %all-gather.2.cloned.1.call-done, bf16[4,256,32]{2,1,0:T(8,128)(2,1)} %get-tuple-element.15, bf16[4,256,32]{2,1,0:T(8,128)(2,1)} %get-tuple-element.14, ...), kind=kOutput, calls=%fused_computation.2 | convolution fusion | flops 4847959040 | bytes 23728128 | tf_op jit(solution)/shard_map/hqc,kc->hqk/dot_general | solution.py:82
  321.1 5.7 %copy-done.1 = f32[4,256,4096]{2,1,0:T(8,128)} copy-done((f32[4,256,4096]{2,1,0:T(8,128)}, f32[4,256,4096]{2,1,0:T(8,128)S(1)}, u32[]{:S(2)}) %copy-start.1) | copy-done | bytes 16777240
  326.8 5.0 %fusion.1 = f32[4,256]{1,0:T(4,128)S(1)} fusion(f32[4,256,4096]{2,1,0:T(8,128)S(1)} %get-tuple-element.23, f32[4,256]{1,0:T(4,128)S(1)} %broadcast_maximum_fusion, pred[256,4096]{1,0:T(8,128)(4,1)S(1)} %copy-done.2), kind=kLoop, calls=%fused_computation.3 | loop fusion | flops 20970496 | bytes 17833984 | tf_op jit(solution)/shard_map/reduce_sum | solution.py:88
  331.8 12.9 %convolution_convert_fusion.2 = bf16[4,256,128]{1,2,0:T(8,128)(2,1)} fusion(bf16[4,512,128]{2,1,0:T(8,128)(2,1)} %param.16, f32[4,256]{1,0:T(4,128)S(1)} %fusion.1, f32[4,256,4096]{2,1,0:T(8,128)} %copy-done.1, f32[4,256]{1,0:T(4,128)S(1)} %broadcast_maximum_fusion, pred[256,4096]{1,0:T(8,128)(4,1)S(1)} %copy-done.2, ...), kind=kOutput, calls=%fused_computation.24 | convolution fusion | flops 4451336192 | bytes 22814720 | tf_op jit(solution)/shard_map/hql,hlv->qhv/dot_general | solution.py:100
  344.8 7.1 %fusion.3 = bf16[7168,256]{0,1:T(8,128)(2,1)} fusion(bf16[256,512]{0,1:T(8,128)(2,1)} %bitcast.34, bf16[512,7168]{1,0:T(8,128)(2,1)} %param.17), kind=kOutput, calls=%fused_computation.6 | convolution fusion | flops 1880883200 | bytes 11272192 | tf_op jit(solution)/shard_map/fc,tf->ct/dot_general | solution.py:105
  351.9 5.9 %copy.39 = bf16[7168,256]{1,0:T(8,128)(2,1)} copy(bf16[7168,256]{0,1:T(8,128)(2,1)} %fusion.3) | data formatting | bytes 7340032
  357.8 4.7 %fusion.16 = bf16[256,576]{0,1:T(8,128)(2,1)} fusion(bf16[4096,576]{0,1:T(8,128)(2,1)} %all-gather.2.cloned.1.call-done, s32[256]{0:T(256)S(1)} %fusion.31), kind=kOutput, calls=%fused_computation.23 | convolution fusion | flops 1209155584 | bytes 5014528 | tf_op jit(solution)/shard_map/dot_general | solution.py:96
  362.5 94.9 %reduce-scatter.4.cloned.1.call-done = bf16[448,256]{1,0:T(8,128)(2,1)} async-done(((bf16[7168,256]{1,0:T(8,128)(2,1)}), bf16[448,256]{1,0:T(8,128)(2,1)}) %reduce-scatter.4.cloned.1.call-update) | async-done | bytes 229392
  (23 shorter events, 0.4 us)
Async XLA Ops:
  7.2 186.8 %copy-start = (bf16[1536,768]{1,0:T(8,128)(2,1)S(1)}, bf16[1536,768]{1,0:T(8,128)(2,1)}, u32[]{:S(2)}) copy-start(bf16[1536,768]{1,0:T(8,128)(2,1)} %param.14) | copy-start | bytes 7077892
  7.2 182.1 %all-reduce.2.cloned.1.call-start = ((), (), s32[]{:S(2)}) async-start(), calls=%async_computation.1 | async-start | bytes 1179648 | tf_op jit(solution)/shard_map/psum | solution.py:73
  9.7 188.8 %copy-start.3 = (s32[32]{0:T(128)S(1)}, s32[32]{0:T(128)}, u32[]{:S(2)}) copy-start(s32[32]{0:T(128)} %param.18) | copy-start | bytes 388
  9.8 300.8 %all-gather.2.cloned.1.call-start = ((), (), s32[]{:S(2)}) async-start(), calls=%async_computation.2 | async-start | bytes 5013504 | tf_op jit(solution)/shard_map/all_gather | solution.py:75
  193.9 263.4 %reduce-scatter.4.cloned.1.call-start = ((), (), s32[]{:S(2)}) async-start(), calls=%async_computation.3 | async-start | bytes 3899392
  310.5 16.3 %copy-start.2 = (pred[256,4096]{1,0:T(8,128)(4,1)S(1)}, pred[256,4096]{1,0:T(8,128)(4,1)}, u32[]{:S(2)}) copy-start(pred[256,4096]{1,0:T(8,128)(4,1)} %broadcast_compare_fusion) | copy-start | bytes 3145732
  321.1 5.7 %copy-start.1 = (f32[4,256,4096]{2,1,0:T(8,128)}, f32[4,256,4096]{2,1,0:T(8,128)S(1)}, u32[]{:S(2)}) copy-start(f32[4,256,4096]{2,1,0:T(8,128)S(1)} %get-tuple-element.23) | copy-start | bytes 50331652
Sparse Core Ops, SparseCore 0:
  10.6 178.5 all-reduce.1
  194.1 116.4 all-gather.1
  357.9 99.3 reduce-scatter.3
where the time goes:
time: 465 us; the launch traced here: 464 us
  waiting for transfers between devices  376 us (81%)
  matrix products  43.3 us (9%)
  local copies, waits for them, and re-layouts  15.4 us (3%)
  other arithmetic  15 us (3%)
  between operations  13.9 us (3%)
    psum x1, waiting for transfers between devices, per_device(): kv_full = lax.psum(partial_value, 'tp')  178 us
    all_gather x1, waiting for transfers between devices, per_device(): kv_piece = lax.all_gather(own_cache, 'ctx', axis=0, tiled=True)  103 us
    unnamed x4, waiting for transfers between devices  94.9 us
    dot_general x1, matrix products, per_device(): jnp.einsum('hql,hlv->qhv', context, w_uv, preferred_element_type=jnp.floa...  12.9 us
    unnamed x9, local copies, waits for them, and re-layouts  11.6 us
    dot_general x1, matrix products, per_device(): jnp.einsum('hqc,kc->hqk', queries, kv_piece, preferred_element_type=jnp.f...  10.5 us
  transfers between devices with their start and end apart: 3, of which 3 were waited for; matrix products, arithmetic and copies ran while one was open for 4% of the time, Pallas kernels for 0%

commit v1 on v0

v1 whole, which is shorter than its diff:
```python
import functools
import math

import jax
import jax.numpy as jnp
from jax import lax
from jax.experimental import pallas as pl
from jax.experimental.pallas import tpu as pltpu
from jax.sharding import PartitionSpec as P

MESH = pl.DeviceIdType.MESH
F32 = jnp.float32
BF16 = jnp.bfloat16
ROWS = 256
HALF = 128
LAT = 512
ROPE = 64
KVW = 576
NOPE = 128
HEADS = 4
MODEL = 7168
BLK = 896
SCALE = 192.0 ** -0.5 * math.log2(math.e)


def dot(a, b):
    return jnp.dot(a, b, preferred_element_type=F32)


def dot_t(a, b):
    return lax.dot_general(a, b, (((1,), (1,)), ((), ())), preferred_element_type=F32)


def rope(v, cos, sin):
    a, b = v[:, :32], v[:, 32:64]
    return jnp.concatenate([a * cos - b * sin, a * sin + b * cos], 1)


def kernel(
    li_hbm, ql_hbm, wdkv_hbm, gain_ref, wuq_hbm, wuk_hbm, wuv_hbm, wo_hbm, order_ref, order_row, slot_row,
    out_ref, own_ref,
    li, ql, wdkv, wuq, wuk, wuv, wo, wo2,
    part, part_recv, ysum, yrecv, zsend, zrecv,
    cos_ref, sin_ref, queries, cache, m_ref, l_ref, acc,
    hv, hv_recv, far_send, far_recv, near_send, near_recv, zo_send, zo_recv, fin, fin_recv,
    ld_sem, wo_ssem, wo_rsem, p_sem, y_sem, z_sem, p1_sem, p2_sem, p3_sem, sh_sem,
    hv_sem, far_sem, near_sem, zo_sem, fin_sem,
):
    c_idx = lax.axis_index("ctx")
    t_idx = lax.axis_index("tp")
    x, zl = c_idx // 4, c_idx % 4
    y, zh, k = t_idx // 4, (t_idx // 2) % 2, t_idx % 2
    z = zh * 4 + zl
    j = 1 - k

    def device(dx=0, dy=0, dz=0, dk=0):
        nx, ny, nz, nk = (x + dx + 4) % 4, (y + dy + 4) % 4, (z + dz + 8) % 8, (k + dk) % 2
        return (nx * 4 + nz % 4, ny * 4 + (nz // 4) * 2 + nk)

    sibling = device(dk=1)

    def remote(src, dst, sem, where):
        copy = pltpu.make_async_remote_copy(
            src_ref=src, dst_ref=dst, send_sem=sem.at[0], recv_sem=sem.at[1],
            device_id=where, device_id_type=MESH,
        )
        return copy

    loads = []
    for i, (src, dst) in enumerate(
        ((li_hbm, li), (wdkv_hbm, wdkv), (ql_hbm, ql), (wuq_hbm, wuq), (wuk_hbm, wuk), (wuv_hbm, wuv), (wo_hbm, wo))
    ):
        loads.append(pltpu.make_async_copy(src, dst, ld_sem.at[i]))
    for copy in loads[:6]:
        copy.start()

    barrier = pltpu.get_barrier_semaphore()
    peers = [
        sibling, device(dy=1), device(dy=-1), device(dy=2), device(dz=4),
        device(dx=1), device(dx=-1), device(dx=2),
        device(dz=1), device(dz=-1), device(dz=2), device(dz=-2),
    ]
    for peer in peers:
        pl.semaphore_signal(barrier, inc=1, device_id=peer, device_id_type=MESH)

    row_id = lax.broadcasted_iota(jnp.int32, (ROWS, 1), 0)
    first, second = order_ref[2 * c_idx] * HALF, order_ref[2 * c_idx + 1] * HALF
    places = jnp.where(row_id < HALF, first + row_id, second + row_id - HALF)

    loads[0].wait()
    loads[1].wait()
    part[pl.ds(j * HALF, HALF), :] = dot(li[pl.ds(pl.multiple_of(j * HALF, HALF), HALF), :], wdkv[...])
    part[pl.ds(k * HALF, HALF), :] = dot(li[pl.ds(pl.multiple_of(k * HALF, HALF), HALF), :], wdkv[...])
    pl.semaphore_wait(barrier, len(peers))
    cp = remote(part.at[pl.ds(pl.multiple_of(j * HALF, HALF), HALF)], part_recv, p_sem, sibling)
    cp.start()

    frequency = jnp.exp(
        lax.broadcasted_iota(jnp.int32, (1, 32), 1).astype(F32) * (-2.0 * math.log(10000.0) / ROPE)
    )
    angles = places.astype(F32) * frequency
    cos_ref[...] = jnp.cos(angles)
    sin_ref[...] = jnp.sin(angles)

    cp.wait()
    ysum[...] = part[pl.ds(pl.multiple_of(k * HALF, HALF), HALF), :] + part_recv[...]
    copies = []
    for i, d in enumerate((1, -1, 2)):
        ny = (y + d + 4) % 4
        cp = remote(
            ysum.at[pl.ds(pl.multiple_of(ny * 32, 32), 32)], yrecv.at[i], y_sem.at[i], device(dy=d)
        )
        cp.start()
        copies.append(cp)
    wo_far = pltpu.make_async_remote_copy(
        src_ref=wo_hbm, dst_ref=wo2, send_sem=wo_ssem, recv_sem=wo_rsem, device_id=sibling, device_id_type=MESH
    )
    wo_far.start()
    loads[6].start()

    loads[2].wait()
    loads[3].wait()
    q_proj = dot(ql[...], wuq[...])
    loads[4].wait()

    def absorb(h):
        q_nope = q_proj[:, 192 * h : 192 * h + NOPE].astype(BF16)
        queries[h, :, :LAT] = dot_t(q_nope, wuk[h]).astype(BF16)
        queries[h, :, LAT:] = rope(
            q_proj[:, 192 * h + NOPE : 192 * h + 192], cos_ref[...], sin_ref[...]
        ).astype(BF16)

    absorb(0)
    absorb(1)
    for cp in copies:
        cp.wait()
    zsend[...] = ((ysum[pl.ds(pl.multiple_of(y * 32, 32), 32), :] + yrecv[0]) + yrecv[1]) + yrecv[2]
    cp = remote(zsend, zrecv, z_sem, device(dz=4))
    cp.start()
    absorb(2)
    absorb(3)
    cp.wait()
    kv = zsend[...] + zrecv[...]
    latent = kv[:, :LAT]
    mean_square = jnp.mean(latent * latent, axis=1, keepdims=True)
    latent = latent * lax.rsqrt(mean_square + 1e-6) * gain_ref[...]
    own_row = pl.multiple_of(k * HALF + y * 32, 32)
    rotated = rope(kv[:, LAT:], cos_ref[pl.ds(own_row, 32), :], sin_ref[pl.ds(own_row, 32), :])

    a_own = x * j + zl * k
    b_own = zl * j + y * k
    c_own = y * j + x * k
    b_sib = zl * k + y * j
    c_sib = y * k + x * j

    def at(core, b, c, a=0, extra=0):
        return pl.multiple_of(core * 2048 + b * 512 + c * 128 + a * 32 + extra, 32)

    own_at = at(k, b_own, c_own, a_own)
    cache[pl.ds(own_at, 32), :] = jnp.concatenate([latent, rotated], 1).astype(BF16)
    own_slab = cache.at[pl.ds(own_at, 32)]
    copies = []
    for i, d in enumerate((1, -1, 2)):
        cp = remote(own_slab, own_slab, p1_sem.at[i], device(dx=d * j, dz=d * k))
        cp.start()
        copies.append(cp)
    for cp in copies:
        cp.wait()

    def group(b, c):
        return cache.at[pl.ds(at(k, b, c), 128)]

    pending = []

    def send_group(r, b):
        mine = group(b, c_own)
        for i, d in enumerate((1, -1, 2)):
            cp = remote(mine, mine, p3_sem.at[r, i], device(dy=d * j, dx=d * k))
            cp.start()
            pending.append(cp)
        cp = remote(mine, mine, sh_sem.at[r, 3], sibling)
        cp.start()
        pending.append(cp)

    mine = group(b_own, c_own)
    half_a = cache.at[pl.ds(at(k, b_own, c_own), 64)]
    half_b = cache.at[pl.ds(at(k, b_own, c_own, 0, 64), 64)]
    second_phase = []
    for i, (src, d) in enumerate(((mine, 1), (mine, -1), (half_a, 2), (half_b, -2))):
        cp = remote(src, src, p2_sem.at[i], device(dz=d * j, dy=d * k))
        cp.start()
        second_phase.append(cp)
    order = [0, 3, 1, 2]
    send_group(0, b_own)
    second_phase[0].wait()
    send_group(1, (b_own + 3) % 4)
    second_phase[1].wait()
    send_group(2, (b_own + 1) % 4)
    second_phase[2].wait()
    second_phase[3].wait()
    send_group(3, (b_own + 2) % 4)

    lane = lax.broadcasted_iota(jnp.int32, (1, 128), 1)

    def bias_of(core, b):
        other = 1 - core
        pieces = []
        for c in range(4):
            held = []
            for a in range(4):
                ctx = (4 * a + b) * other + (4 * c + a) * core
                held.append(order_ref[2 * ctx + core] * HALF)
            base = jnp.where(
                lane < 64, jnp.where(lane < 32, held[0], held[1]), jnp.where(lane < 96, held[2], held[3])
            )
            pieces.append(base + lane % 32 + 32 * (c * other + b * core))
        key_places = jnp.concatenate(pieces, 1)
        return jnp.where(key_places <= places, 0.0, -1e30)

    m_ref[...] = jnp.full(m_ref.shape, -1e29, F32)
    l_ref[...] = jnp.zeros(l_ref.shape, F32)
    acc[...] = jnp.zeros(acc.shape, F32)

    def attend(core, b):
        bias = bias_of(core, b)
        rows = pl.ds(at(core, b, 0), 512)

        def heads(i, carry):
            for u in range(2):
                h = 2 * i + u
                scores = dot_t(queries[h], cache[rows, :]) * SCALE + bias
                m_old = m_ref[h]
                m_new = jnp.maximum(m_old, jnp.max(scores, axis=1, keepdims=True))
                alpha = jnp.exp2(m_old - m_new)
                probs = jnp.exp2(scores - m_new[:, :1])
                l_ref[h] = l_ref[h] * alpha + jnp.sum(probs, axis=1, keepdims=True)
                m_ref[h] = m_new
                acc[h] = acc[h] * alpha[:, :1] + dot(probs.astype(BF16), cache[rows, :LAT])
            return carry

        lax.fori_loop(0, 2, heads, 0)

    for r in range(4):
        b = (b_own + order[r]) % 4
        for i, d in enumerate((1, -1, 2)):
            remote(mine, mine, p3_sem.at[r, i], sibling).wait_recv()
            got = group(b, (c_own - d + 4) % 4)
            cp = remote(got, got, sh_sem.at[r, i], sibling)
            cp.start()
            pending.append(cp)
        attend(k, b)
        for i in range(4):
            remote(mine, mine, sh_sem.at[r, i], sibling).wait_recv()
        attend(j, (b_sib + order[r]) % 4)

    loads[5].wait()
    for h in range(HEADS):
        context = (acc[h] / l_ref[h][:, :1]).astype(BF16)
        hv[:, 128 * h : 128 * (h + 1)] = dot(context, wuv[h]).astype(BF16)
    hv_copy = remote(hv.at[pl.ds(pl.multiple_of(j * HALF, HALF), HALF)], hv_recv, hv_sem, sibling)
    hv_copy.start()

    number = lax.broadcasted_iota(jnp.int32, (1, 32), 1)
    sources = []
    for i in range(2):
        prompt = jnp.sum(jnp.where(slot_row[...] == 2 * c_idx + i, number, 0), axis=1, keepdims=True)
        held = jnp.sum(jnp.where(order_row[...] == prompt, number, 0), axis=1, keepdims=True)
        core, hx, hz = held & 1, held >> 3, (held >> 1) & 3
        row = row_id[:HALF]
        q, rest = row >> 5, row & 31
        zero = hz * 512 + q * 128 + hx * 32 + rest
        one = 2048 + q * 512 + hx * 128 + hz * 32 + rest
        sources.append(jnp.where(core == 0, zero, one))
    source = jnp.concatenate(sources, 0)
    key_lane = lax.broadcasted_iota(jnp.int32, (1, 1024), 1)
    picked_rows = jnp.zeros((ROWS, KVW), F32)
    for n in range(4):
        picked = jnp.where(key_lane + 1024 * n == source, 1.0, 0.0).astype(BF16)
        picked_rows = picked_rows + dot(picked, cache[1024 * n : 1024 * (n + 1), :])
    own_ref[...] = picked_rows.astype(BF16)

    loads[6].wait()
    wo_far.wait()
    hv_copy.wait()
    hv_own_rows = pl.ds(pl.multiple_of(k * HALF, HALF), HALF)

    def partial(dy, zz):
        columns = pl.ds(pl.multiple_of((((y + dy + 4) % 4) * 2 + zz) * BLK, 128), BLK)
        return dot(hv[hv_own_rows, :], wo[:, columns]) + dot(hv_recv[...], wo2[:, columns])

    up, down = device(dy=1), device(dy=-1)
    near = {}
    sides = ((0, 1 - zh), (1, zh))
    far = {}
    for s, zz in sides:
        p = partial(2, zz).astype(BF16)
        for i, where in enumerate((up, down)):
            far_send[s, i] = p[64 * i : 64 * (i + 1)]
            cp = remote(far_send.at[s, i], far_recv.at[s, i], far_sem.at[s, i], where)
            cp.start()
            far[s, i] = cp
        for e, (dy, where) in enumerate(((1, up), (-1, down))):
            p = partial(dy, zz)
            near_send[s, e, 1 - e] = p[64 * (1 - e) : 64 * (2 - e)].astype(BF16)
            cp = remote(near_send.at[s, e, 1 - e], near_recv.at[s, e, 1 - e], near_sem.at[s, e, 1 - e], where)
            cp.start()
            near[s, e, 1 - e] = cp
            far[s, e].wait()
            near_send[s, e, e] = (p[64 * e : 64 * (e + 1)] + far_recv[s, e].astype(F32)).astype(BF16)
            cp = remote(near_send.at[s, e, e], near_recv.at[s, e, e], near_sem.at[s, e, e], where)
            cp.start()
            near[s, e, e] = cp
    for s, zz in sides:
        p = partial(0, zz)
        for e in range(2):
            for f in range(2):
                near[s, e, f].wait()
        total = p + (
            jnp.concatenate([near_recv[s, 0, 0], near_recv[s, 0, 1]], 0).astype(F32)
            + jnp.concatenate([near_recv[s, 1, 0], near_recv[s, 1, 1]], 0).astype(F32)
        )
        if s == 0:
            zo_send[...] = total.astype(BF16)
            zo_copy = remote(zo_send, zo_recv, zo_sem, device(dz=4))
            zo_copy.start()
    zo_copy.wait()
    fin[...] = (total + zo_recv[...].astype(F32)).astype(BF16)
    fin_copy = remote(fin, fin_recv, fin_sem, sibling)
    fin_copy.start()
    mine_here = fin[...]
    out_ref[hv_own_rows, :] = jnp.where(k == 0, mine_here[:, :448], mine_here[:, 448:])
    fin_copy.wait()
    theirs = fin_recv[...]
    out_ref[pl.ds(pl.multiple_of(j * HALF, HALF), HALF), :] = jnp.where(k == 0, theirs[:, :448], theirs[:, 448:])
    for cp in pending:
        cp.wait_send()


def per_device(
    layer_input, q_latent, w_dkv, kv_gain, w_uq, w_uk, w_uv, w_o, block_order, owner_slot
):
    hbm = pl.BlockSpec(memory_space=pl.ANY)
    vmem = pl.BlockSpec(memory_space=pltpu.VMEM)
    smem = pl.BlockSpec(memory_space=pltpu.SMEM)
    V = pltpu.VMEM
    dma = pltpu.SemaphoreType.DMA
    return pl.pallas_call(
        kernel,
        out_shape=(
            jax.ShapeDtypeStruct((ROWS, 448), BF16),
            jax.ShapeDtypeStruct((ROWS, KVW), BF16),
        ),
        in_specs=[hbm, hbm, hbm, vmem, hbm, hbm, hbm, hbm, smem, vmem, vmem],
        out_specs=(vmem, vmem),
        scratch_shapes=[
            V((ROWS, 448), BF16), V((ROWS, 1536), BF16), V((448, KVW), BF16), V((1536, 768), BF16),
            V((HEADS, LAT, NOPE), BF16), V((HEADS, LAT, NOPE), BF16), V((512, MODEL), BF16), V((512, MODEL), BF16),
            V((ROWS, KVW), F32), V((HALF, KVW), F32), V((HALF, KVW), F32), V((3, 32, KVW), F32),
            V((32, KVW), F32), V((32, KVW), F32),
            V((ROWS, 32), F32), V((ROWS, 32), F32), V((HEADS, ROWS, KVW), BF16), V((4096, KVW), BF16),
            V((HEADS, ROWS, 128), F32), V((HEADS, ROWS, 128), F32), V((HEADS, ROWS, LAT), F32),
            V((ROWS, 512), BF16), V((HALF, 512), BF16),
            V((2, 2, 64, BLK), BF16), V((2, 2, 64, BLK), BF16),
            V((2, 2, 2, 64, BLK), BF16), V((2, 2, 2, 64, BLK), BF16),
            V((HALF, BLK), BF16), V((HALF, BLK), BF16), V((HALF, BLK), BF16), V((HALF, BLK), BF16),
            dma((7,)), dma, dma, dma((2,)), dma((3, 2)), dma((2,)), dma((3, 2)), dma((4, 2)),
            dma((4, 3, 2)), dma((4, 4, 2)), dma((2,)), dma((2, 2, 2)), dma((2, 2, 2, 2)), dma((2,)), dma((2,)),
        ],
        compiler_params=pltpu.CompilerParams(
            collective_id=0, has_side_effects=True, vmem_limit_bytes=60 * 1024 * 1024
        ),
    )(
        layer_input, q_latent, w_dkv, kv_gain.reshape(1, LAT), w_uq, w_uk, w_uv, w_o,
        block_order, block_order.reshape(1, 32), owner_slot.reshape(1, 32),
    )


def solution(mesh):
    return jax.shard_map(
        per_device,
        mesh=mesh,
        in_specs=(
            P("ctx", "tp"),
            P("ctx", None),
            P("tp", None),
            P(),
            P(None, "tp"),
            P("tp", None, None),
            P("tp", None, None),
            P("tp", None),
            P(),
            P(),
        ),
        out_specs=(P("ctx", "tp"), P("ctx", None)),
        check_vma=False,
    )
```

time: 465 us -> 102 us (0.22)
  waiting for transfers between devices: 376 us -> 0 us
  Pallas kernels: 0 us -> 95.6 us
  matrix products: 43.3 us -> 0 us
  other arithmetic: 15 us -> 0 us
  between operations: 13.9 us -> 0.64 us
  local copies, waits for them, and re-layouts: 15.4 us -> 5.4 us
    psum x1 -> x0, waiting for transfers between devices: 178 us -> none  [per_device(): kv_full = lax.psum(partial_value, 'tp')]
    all_gather x1 -> x0, waiting for transfers between devices: 103 us -> none  [per_device(): kv_piece = lax.all_gather(own_cache, 'ctx', axis=0, tiled=True)]
    pallas_call x0 -> x1, Pallas kernels: none -> 95.6 us  [per_device(): pl.pallas_call(kernel, out_shape=(jax.ShapeDtypeStruct((ROWS, 448), BF16)...]
    unnamed x4 -> x0, waiting for transfers between devices: 94.9 us -> none
    dot_general x7 -> x0, matrix products: 43.3 us -> none  [the longest x1 12.9 us: per_device(): jnp.einsum('hql,hlv->qhv', context, w_uv, preferred_element_type=jnp.floa...]
    unnamed x9 -> x1, local copies, waits for them, and re-layouts: 11.6 us -> 1.78 us
    reduce_sum x5 -> x0, other arithmetic: 7.8 us -> none  [the longest x1 5.03 us: per_device(): l_new = jnp.sum(weights, axis=2)]
  transfers between devices with their start and end apart: 3 -> 0, of which waited for: 3 -> 0; matrix products, arithmetic and copies ran while one was open for 4% -> 0% of each run, Pallas kernels for 0% -> 0%
where the time goes in v1:
time: 102 us
  Pallas kernels  95.6 us (94%)
  local copies, waits for them, and re-layouts  5.4 us (5%)
    pallas_call x1, Pallas kernels, per_device(): pl.pallas_call(kernel, out_shape=(jax.ShapeDtypeStruct((ROWS, 448), BF16)...  95.6 us
    pallas_call x2, local copies, waits for them, and re-layouts, per_device(): pl.pallas_call(kernel, out_shape=(jax.ShapeDtypeStruct((ROWS, 448), BF16)...  3.62 us

profile of v1, /device:TPU:1, one launch (start us, length us, event | category | flops | bytes accessed | tf_op | source)
XLA Modules:
  0.0 101.6 jit_solution(5464796633062046992)
XLA Ops:
  0.6 1.8 %copy.12.li_hbm = bf16[256,448]{1,0:T(8,128)(2,1)} copy(bf16[256,448]{0,1:T(8,128)(2,1)} %param.10) | data formatting | bytes 458752 | tf_op args[0]
  2.4 95.6 %shard_map.113 = (bf16[256,448]{1,0:T(8,128)(2,1)}, bf16[256,576]{1,0:T(8,128)(2,1)}) custom-call(bf16[256,448]{1,0:T(8,128)(2,1)} %copy.12.li_hbm, bf16[256,1536]{1,0:T(8,128)(2,1)} %ql_hbm.1, bf16[448,576]{1,0:T(8,128)(2,1)} %wdkv_hbm.1, f32[1,512]{1,0:T(1,128)} %bitcast.4, bf16[1536,768]{1,0:T(8,128)(2,1)} %wuq_hbm.1, bf16[4,512,128]{2,1,0:T(8,128)(2,1)} %wuk_hbm.1, ...), custom_call_target="tpu_custom_call" | custom-call | tf_op jit(solution)/shard_map/pallas_call | solution.py:347
  98.0 1.8 %copy.13 = bf16[256,448]{0,1:T(8,128)(2,1)} copy(bf16[256,448]{1,0:T(8,128)(2,1)} %get-tuple-element.2) | data formatting | bytes 458752 | tf_op jit(solution)/shard_map/pallas_call | solution.py:347
  99.8 1.8 %copy.14 = bf16[256,576]{0,1:T(8,128)(2,1)} copy(bf16[256,576]{1,0:T(8,128)(2,1)} %get-tuple-element.3) | data formatting | bytes 589824 | tf_op jit(solution)/shard_map/pallas_call | solution.py:347

commit v2 on v1

v2 whole, which is shorter than its diff:
```python
import functools
import math

import jax
import jax.numpy as jnp
from jax import lax
from jax.experimental import pallas as pl
from jax.experimental.pallas import tpu as pltpu
from jax.sharding import PartitionSpec as P

MESH = pl.DeviceIdType.MESH
F32 = jnp.float32
BF16 = jnp.bfloat16
ROWS = 256
HALF = 128
LAT = 512
ROPE = 64
KVW = 576
NOPE = 128
HEADS = 4
MODEL = 7168
BLK = 896
SCALE = 192.0 ** -0.5 * math.log2(math.e)


def dot(a, b):
    return jnp.dot(a, b, preferred_element_type=F32)


def dot_t(a, b):
    return lax.dot_general(a, b, (((1,), (1,)), ((), ())), preferred_element_type=F32)


def rope(v, cos, sin):
    a, b = v[:, :32], v[:, 32:64]
    return jnp.concatenate([a * cos - b * sin, a * sin + b * cos], 1)


def kernel(
    li_hbm, ql_hbm, wdkv_hbm, gain_ref, wuq_hbm, wuk_hbm, wuv_hbm, wo_hbm, order_ref, order_row, slot_row,
    out_ref, own_ref,
    li, ql, wdkv, wuq, wuk, wuv, wo, wo2,
    part, part_recv, ysum, yrecv, zsend, zrecv,
    cos_ref, sin_ref, queries, cache, m_ref, l_ref, acc,
    hv, hv_recv, far_send, far_recv, near_send, near_recv, zo_send, zo_recv, fin, fin_recv,
    ld_sem, wo_ssem, wo_rsem, p_sem, y_sem, z_sem, p1_sem, p2_sem, p3_sem, p4_sem, sh_sem,
    hv_sem, far_sem, near_sem, zo_sem, fin_sem,
):
    c_idx = lax.axis_index("ctx")
    t_idx = lax.axis_index("tp")
    x, zl = c_idx // 4, c_idx % 4
    y, zh, k = t_idx // 4, (t_idx // 2) % 2, t_idx % 2
    z = zh * 4 + zl
    j = 1 - k

    def device(dx=0, dy=0, dz=0, dk=0):
        nx, ny, nz, nk = (x + dx + 4) % 4, (y + dy + 4) % 4, (z + dz + 8) % 8, (k + dk) % 2
        return (nx * 4 + nz % 4, ny * 4 + (nz // 4) * 2 + nk)

    sibling = device(dk=1)

    def remote(src, dst, sem, where):
        copy = pltpu.make_async_remote_copy(
            src_ref=src, dst_ref=dst, send_sem=sem.at[0], recv_sem=sem.at[1],
            device_id=where, device_id_type=MESH,
        )
        return copy

    loads = []
    for i, (src, dst) in enumerate(
        ((li_hbm, li), (wdkv_hbm, wdkv), (ql_hbm, ql), (wuq_hbm, wuq), (wuk_hbm, wuk), (wuv_hbm, wuv), (wo_hbm, wo))
    ):
        loads.append(pltpu.make_async_copy(src, dst, ld_sem.at[i]))
    for copy in loads[:6]:
        copy.start()

    barrier = pltpu.get_barrier_semaphore()
    peers = [
        sibling, device(dy=1), device(dy=-1), device(dy=2), device(dz=4),
        device(dx=1), device(dx=-1), device(dx=2),
        device(dz=1), device(dz=-1), device(dz=2), device(dz=-2),
    ]
    for peer in peers:
        pl.semaphore_signal(barrier, inc=1, device_id=peer, device_id_type=MESH)

    row_id = lax.broadcasted_iota(jnp.int32, (ROWS, 1), 0)
    first, second = order_ref[2 * c_idx] * HALF, order_ref[2 * c_idx + 1] * HALF
    places = jnp.where(row_id < HALF, first + row_id, second + row_id - HALF)

    loads[0].wait()
    loads[1].wait()
    part[...] = lax.dot_general(li[...], wdkv[...], (((0,), (0,)), ((), ())), preferred_element_type=F32)
    pl.semaphore_wait(barrier, len(peers))
    cp = remote(part.at[pl.ds(pl.multiple_of(j * HALF, HALF), HALF)], part_recv, p_sem, sibling)
    cp.start()

    frequency = jnp.exp(
        lax.broadcasted_iota(jnp.int32, (1, 32), 1).astype(F32) * (-2.0 * math.log(10000.0) / ROPE)
    )
    angles = places.astype(F32) * frequency
    cos_ref[...] = jnp.cos(angles)
    sin_ref[...] = jnp.sin(angles)

    cp.wait()
    ysum[...] = part[pl.ds(pl.multiple_of(k * HALF, HALF), HALF), :] + part_recv[...]
    copies = []
    for i, d in enumerate((1, -1, 2)):
        ny = (y + d + 4) % 4
        cp = remote(
            ysum.at[pl.ds(pl.multiple_of(ny * 32, 32), 32)], yrecv.at[i], y_sem.at[i], device(dy=d)
        )
        cp.start()
        copies.append(cp)
    wo_far = pltpu.make_async_remote_copy(
        src_ref=wo_hbm, dst_ref=wo2, send_sem=wo_ssem, recv_sem=wo_rsem, device_id=sibling, device_id_type=MESH
    )
    wo_far.start()
    loads[6].start()

    loads[2].wait()
    loads[3].wait()
    q_proj = dot(ql[...], wuq[...])
    loads[4].wait()

    def absorb(h):
        q_nope = q_proj[:, 192 * h : 192 * h + NOPE].astype(BF16)
        queries[h, :, :LAT] = dot_t(q_nope, wuk[h]).astype(BF16)
        queries[h, :, LAT:] = rope(
            q_proj[:, 192 * h + NOPE : 192 * h + 192], cos_ref[...], sin_ref[...]
        ).astype(BF16)

    absorb(0)
    absorb(1)
    for cp in copies:
        cp.wait()
    zsend[...] = ((ysum[pl.ds(pl.multiple_of(y * 32, 32), 32), :] + yrecv[0]) + yrecv[1]) + yrecv[2]
    cp = remote(zsend, zrecv, z_sem, device(dz=4))
    cp.start()
    absorb(2)
    absorb(3)
    cp.wait()
    kv = zsend[...] + zrecv[...]
    latent = kv[:, :LAT]
    mean_square = jnp.mean(latent * latent, axis=1, keepdims=True)
    latent = latent * lax.rsqrt(mean_square + 1e-6) * gain_ref[...]
    own_row = pl.multiple_of(k * HALF + y * 32, 32)
    rotated = rope(kv[:, LAT:], cos_ref[pl.ds(own_row, 32), :], sin_ref[pl.ds(own_row, 32), :])

    a_own = x * j + y * k
    c_own = y * j + x * k

    def at(core, b, c, a=0, extra=0):
        return pl.multiple_of(core * 2048 + b * 512 + c * 128 + a * 32 + extra, 32)

    own_at = at(k, zl, c_own, a_own)
    cache[pl.ds(own_at, 32), :] = jnp.concatenate([latent, rotated], 1).astype(BF16)
    own_slab = cache.at[pl.ds(own_at, 32)]
    copies = []
    for i, d in enumerate((1, -1, 2)):
        cp = remote(own_slab, own_slab, p1_sem.at[i], device(dx=d * j, dy=d * k))
        cp.start()
        copies.append(cp)
    for cp in copies:
        cp.wait()

    def group(b, c):
        return cache.at[pl.ds(at(k, b, c), 128)]

    def half(b, c, e):
        return cache.at[pl.ds(at(k, b, c, 0, 64 * e), 64)]

    c_up, c_down = device(dy=j, dx=k), device(dy=-j, dx=-k)
    mine = group(zl, c_own)
    mine_half = half(zl, c_own, 0)

    def share(r, i, src):
        remote(src, src, sh_sem.at[r, i], sibling).start()

    def send_group(r, b):
        src = group(b, c_own)
        remote(src, src, p3_sem.at[r, 0], c_up).start()
        remote(src, src, p3_sem.at[r, 1], c_down).start()
        share(r, 3, src)

    def near_groups(r, b):
        below, above = (c_own + 3) % 4, (c_own + 1) % 4
        remote(mine, mine, p3_sem.at[r, 0], sibling).wait_recv()
        src = half(b, below, 0)
        remote(src, src, p4_sem.at[r, 0], c_up).start()
        share(r, 0, group(b, below))
        remote(mine, mine, p3_sem.at[r, 1], sibling).wait_recv()
        src = half(b, above, 1)
        remote(src, src, p4_sem.at[r, 1], c_down).start()
        share(r, 1, group(b, above))

    def far_group(r, b):
        for e in range(2):
            remote(mine_half, mine_half, p4_sem.at[r, e], sibling).wait_recv()
        share(r, 2, group(b, (c_own + 2) % 4))

    def shared(r):
        for i in range(4):
            remote(mine, mine, sh_sem.at[r, i], sibling).wait_recv()

    second_phase = []
    for i, (src, d) in enumerate(((mine, 1), (mine, -1), (half(zl, c_own, 0), 2), (half(zl, c_own, 1), -2))):
        cp = remote(src, src, p2_sem.at[i], device(dz=d))
        cp.start()
        second_phase.append(cp)

    lane = lax.broadcasted_iota(jnp.int32, (1, 128), 1)

    def bias_of(core, b):
        other = 1 - core
        pieces = []
        for c in range(4):
            held = []
            for a in range(4):
                ctx = 4 * (a * other + c * core) + b
                held.append(order_ref[2 * ctx + core] * HALF)
            base = jnp.where(
                lane < 64, jnp.where(lane < 32, held[0], held[1]), jnp.where(lane < 96, held[2], held[3])
            )
            pieces.append(base + lane % 32 + 32 * c * other + (lane // 32) * 32 * core)
        key_places = jnp.concatenate(pieces, 1)
        return jnp.where(key_places <= places, 0.0, -1e30)

    m_ref[...] = jnp.full(m_ref.shape, -1e29, F32)
    l_ref[...] = jnp.zeros(l_ref.shape, F32)
    acc[...] = jnp.zeros(acc.shape, F32)

    def attend(core, b):
        bias = bias_of(core, b)
        rows = pl.ds(at(core, b, 0), 512)

        def add_product(h, alpha, probs):
            acc[h] = acc[h] * alpha + dot(probs, cache[rows, :LAT])

        scores_next = dot_t(queries[0], cache[rows, :])
        last = None
        for h in range(HEADS):
            scores = scores_next
            if h + 1 < HEADS:
                scores_next = dot_t(queries[h + 1], cache[rows, :])
            if last is not None:
                add_product(*last)
            scores = scores * SCALE + bias
            m_old = m_ref[h]
            m_new = jnp.maximum(m_old, jnp.max(scores, axis=1, keepdims=True))
            alpha = jnp.exp2(m_old - m_new)
            probs = jnp.exp2(scores - m_new[:, :1])
            l_ref[h] = l_ref[h] * alpha + jnp.sum(probs, axis=1, keepdims=True)
            m_ref[h] = m_new
            last = (h, alpha[:, :1], probs.astype(BF16))
        add_product(*last)

    def place_of(r):
        return (zl + 3 - 2 * (r - 1) + 3 * ((r - 1) * (r - 2) // 2)) % 4

    send_group(0, zl)
    second_phase[0].wait()
    send_group(1, place_of(1))
    second_phase[1].wait()
    send_group(2, place_of(2))
    near_groups(0, zl)
    far_group(0, zl)
    attend(k, zl)
    second_phase[2].wait()
    second_phase[3].wait()
    send_group(3, place_of(3))

    def round_of(r, b_last):
        b = place_of(r)
        near_groups(r, b)
        shared(r - 1)
        attend(j, b_last)
        far_group(r, b)
        attend(k, b)
        return b

    b_last = lax.fori_loop(1, 4, round_of, zl)
    shared(3)
    attend(j, b_last)

    loads[5].wait()
    for h in range(HEADS):
        context = (acc[h] / l_ref[h][:, :1]).astype(BF16)
        hv[:, 128 * h : 128 * (h + 1)] = dot(context, wuv[h]).astype(BF16)
    hv_copy = remote(hv.at[pl.ds(pl.multiple_of(j * HALF, HALF), HALF)], hv_recv, hv_sem, sibling)
    hv_copy.start()

    number = lax.broadcasted_iota(jnp.int32, (1, 32), 1)
    sources = []
    for i in range(2):
        prompt = jnp.sum(jnp.where(slot_row[...] == 2 * c_idx + i, number, 0), axis=1, keepdims=True)
        held = jnp.sum(jnp.where(order_row[...] == prompt, number, 0), axis=1, keepdims=True)
        core, hx, hz = held & 1, held >> 3, (held >> 1) & 3
        row = row_id[:HALF]
        q, rest = row >> 5, row & 31
        zero = hz * 512 + q * 128 + hx * 32 + rest
        one = 2048 + hz * 512 + hx * 128 + q * 32 + rest
        sources.append(jnp.where(core == 0, zero, one))
    source = jnp.concatenate(sources, 0)
    key_lane = lax.broadcasted_iota(jnp.int32, (1, 1024), 1)
    picked_rows = jnp.zeros((ROWS, KVW), F32)
    for n in range(4):
        picked = jnp.where(key_lane + 1024 * n == source, 1.0, 0.0).astype(BF16)
        picked_rows = picked_rows + dot(picked, cache[1024 * n : 1024 * (n + 1), :])
    own_ref[...] = picked_rows.T.astype(BF16)

    loads[6].wait()
    wo_far.wait()
    hv_copy.wait()
    hv_own_rows = pl.ds(pl.multiple_of(k * HALF, HALF), HALF)

    up, down = device(dy=1), device(dy=-1)
    chunks = ((0, 0, 256), (0, 256, 256), (0, 512, 384), (1, 0, 512), (1, 512, 384))

    def partial(dy, n):
        s, first_column, width = chunks[n]
        zz = (1 - zh) * (1 - s) + zh * s
        start = (((y + dy + 4) % 4) * 2 + zz) * BLK + first_column
        columns = pl.ds(pl.multiple_of(start, 128), width)
        return dot(hv[hv_own_rows, :], wo[:, columns]) + dot(hv_recv[...], wo2[:, columns])

    def span(ref, n):
        s, first_column, width = chunks[n]
        return ref.at[s, :, pl.ds(first_column, width)]

    def far_out(n):
        p = partial(2, n).astype(BF16)
        for e, where in enumerate((up, down)):
            src = span(far_send.at[e], n)
            src[...] = p[64 * e : 64 * (e + 1)]
            remote(src, span(far_recv.at[e], n), far_sem.at[n, e], where).start()

    def near_copy(n, e, f, where):
        return remote(span(near_send.at[e, f], n), span(near_recv.at[e, f], n), near_sem.at[n, e, f], where)

    held = {}

    def near_out(n):
        for e, (dy, where) in enumerate(((1, up), (-1, down))):
            p = partial(dy, n)
            f = 1 - e
            span(near_send.at[e, f], n)[...] = p[64 * f : 64 * (f + 1)].astype(BF16)
            near_copy(n, e, f, where).start()
            held[n, e] = p[64 * e : 64 * (e + 1)]

    def near_added(n):
        for e, where in enumerate((up, down)):
            remote(span(far_send.at[e], n), span(far_recv.at[e], n), far_sem.at[n, e], where).wait()
            span(near_send.at[e, e], n)[...] = (
                held[n, e] + span(far_recv.at[e], n)[...].astype(F32)
            ).astype(BF16)
            near_copy(n, e, e, where).start()

    z_copies = []

    def finish(n):
        s, first_column, width = chunks[n]
        columns = pl.ds(first_column, width)
        p = partial(0, n)
        for e, where in enumerate((up, down)):
            for f in range(2):
                near_copy(n, e, f, where).wait()
        sums = [
            span(near_recv.at[0, f], n)[...].astype(F32) + span(near_recv.at[1, f], n)[...].astype(F32)
            for f in range(2)
        ]
        total = p + jnp.concatenate(sums, 0)
        if s == 0:
            zo_send[:, columns] = total.astype(BF16)
            cp = remote(zo_send.at[:, columns], zo_recv.at[:, columns], zo_sem.at[n], device(dz=4))
            cp.start()
            z_copies.append(cp)
            return
        for cp in z_copies[:2] if n == 3 else z_copies[2:]:
            cp.wait()
        fin[:, columns] = (total + zo_recv[:, columns].astype(F32)).astype(BF16)
        fin_copy(n).start()

    def fin_copy(n):
        columns = pl.ds(chunks[n][1], chunks[n][2])
        return remote(fin.at[:, columns], fin_recv.at[:, columns], fin_sem.at[n - 3], sibling)

    far_out(0)
    near_out(0)
    far_out(1)
    near_added(0)
    near_out(1)
    far_out(2)
    near_added(1)
    near_out(2)
    finish(0)
    far_out(3)
    near_added(2)
    near_out(3)
    finish(1)
    far_out(4)
    near_added(3)
    near_out(4)
    finish(2)
    near_added(4)
    finish(3)
    finish(4)
    mine_here = fin[...]
    mine_here = jnp.where(k == 0, mine_here[:, :448], mine_here[:, 448:])
    out_ref[:, hv_own_rows] = mine_here.T
    fin_copy(3).wait()
    fin_copy(4).wait()
    theirs = fin_recv[...]
    theirs = jnp.where(k == 0, theirs[:, :448], theirs[:, 448:])
    out_ref[:, pl.ds(pl.multiple_of(j * HALF, HALF), HALF)] = theirs.T
    for r in range(4):
        for i in range(2):
            remote(mine, mine, p3_sem.at[r, i], sibling).wait_send()
            remote(mine_half, mine_half, p4_sem.at[r, i], sibling).wait_send()
        for i in range(4):
            remote(mine, mine, sh_sem.at[r, i], sibling).wait_send()


def per_device(
    layer_input, q_latent, w_dkv, kv_gain, w_uq, w_uk, w_uv, w_o, block_order, owner_slot
):
    hbm = pl.BlockSpec(memory_space=pl.ANY)
    vmem = pl.BlockSpec(memory_space=pltpu.VMEM)
    smem = pl.BlockSpec(memory_space=pltpu.SMEM)
    V = pltpu.VMEM
    dma = pltpu.SemaphoreType.DMA
    out, own = pl.pallas_call(
        kernel,
        out_shape=(
            jax.ShapeDtypeStruct((448, ROWS), BF16),
            jax.ShapeDtypeStruct((KVW, ROWS), BF16),
        ),
        in_specs=[hbm, hbm, hbm, vmem, hbm, hbm, hbm, hbm, smem, vmem, vmem],
        out_specs=(vmem, vmem),
        scratch_shapes=[
            V((448, ROWS), BF16), V((ROWS, 1536), BF16), V((448, KVW), BF16), V((1536, 768), BF16),
            V((HEADS, LAT, NOPE), BF16), V((HEADS, LAT, NOPE), BF16), V((512, MODEL), BF16), V((512, MODEL), BF16),
            V((ROWS, KVW), F32), V((HALF, KVW), F32), V((HALF, KVW), F32), V((3, 32, KVW), F32),
            V((32, KVW), F32), V((32, KVW), F32),
            V((ROWS, 32), F32), V((ROWS, 32), F32), V((HEADS, ROWS, KVW), BF16), V((4096, KVW), BF16),
            V((HEADS, ROWS, 128), F32), V((HEADS, ROWS, 128), F32), V((HEADS, ROWS, LAT), F32),
            V((ROWS, 512), BF16), V((HALF, 512), BF16),
            V((2, 2, 64, BLK), BF16), V((2, 2, 64, BLK), BF16),
            V((2, 2, 2, 64, BLK), BF16), V((2, 2, 2, 64, BLK), BF16),
            V((HALF, BLK), BF16), V((HALF, BLK), BF16), V((HALF, BLK), BF16), V((HALF, BLK), BF16),
            dma((7,)), dma, dma, dma((2,)), dma((3, 2)), dma((2,)), dma((3, 2)), dma((4, 2)),
            dma((4, 2, 2)), dma((4, 2, 2)), dma((4, 4, 2)), dma((2,)), dma((5, 2, 2)), dma((5, 2, 2, 2)),
            dma((3, 2)), dma((2, 2)),
        ],
        compiler_params=pltpu.CompilerParams(
            collective_id=0, has_side_effects=True, vmem_limit_bytes=60 * 1024 * 1024
        ),
    )(
        layer_input.T, q_latent, w_dkv, kv_gain.reshape(1, LAT), w_uq, w_uk, w_uv, w_o,
        block_order, block_order.reshape(1, 32), owner_slot.reshape(1, 32),
    )
    return out.T, own.T


def solution(mesh):
    return jax.shard_map(
        per_device,
        mesh=mesh,
        in_specs=(
            P("ctx", "tp"),
            P("ctx", None),
            P("tp", None),
            P(),
            P(None, "tp"),
            P("tp", None, None),
            P("tp", None, None),
            P("tp", None),
            P(),
            P(),
        ),
        out_specs=(P("ctx", "tp"), P("ctx", None)),
        check_vma=False,
    )
```

time: 102 us -> 94.9 us (0.930)
  Pallas kernels: 95.6 us -> 90.7 us
  local copies, waits for them, and re-layouts: 5.4 us -> 3.33 us
    pallas_call x1, Pallas kernels: 95.6 us -> 90.7 us  [per_device(): pl.pallas_call(kernel, out_shape=(jax.ShapeDtypeStruct((448, ROWS), BF16)...]
    pallas_call x2 -> x0, local copies, waits for them, and re-layouts: 3.62 us -> none  [per_device(): pl.pallas_call(kernel, out_shape=(jax.ShapeDtypeStruct((ROWS, 448), BF16)...]
    unnamed x1 -> x2, local copies, waits for them, and re-layouts: 1.78 us -> 3.33 us
where the time goes in v2:
time: 94.9 us; the launch traced here: 94.7 us
  Pallas kernels  90.7 us (96%)
  local copies, waits for them, and re-layouts  3.33 us (4%)
    pallas_call x1, Pallas kernels, per_device(): pl.pallas_call(kernel, out_shape=(jax.ShapeDtypeStruct((448, ROWS), BF16)...  90.7 us
    unnamed x2, local copies, waits for them, and re-layouts  3.33 us

profile of v2, /device:TPU:1, one launch (start us, length us, event | category | flops | bytes accessed | tf_op | source)
XLA Modules:
  0.0 94.7 jit_solution(16866743691383539237)
XLA Ops:
  0.6 90.7 %shard_map.113 = (bf16[448,256]{1,0:T(8,128)(2,1)}, bf16[576,256]{1,0:T(8,128)(2,1)}) custom-call(bf16[448,256]{1,0:T(8,128)(2,1)} %bitcast.8, bf16[256,1536]{1,0:T(8,128)(2,1)} %ql_hbm.1, bf16[448,576]{1,0:T(8,128)(2,1)} %wdkv_hbm.1, f32[1,512]{1,0:T(1,128)} %bitcast.10, bf16[1536,768]{1,0:T(8,128)(2,1)} %wuq_hbm.1, bf16[4,512,128]{2,1,0:T(8,128)(2,1)} %wuk_hbm.1, ...), custom_call_target="tpu_custom_call" | custom-call | tf_op jit(solution)/shard_map/pallas_call | solution.py:431
  91.3 1.6 %copy.14 = bf16[256,448]{0,1:T(8,128)(2,1)} copy(bf16[256,448]{0,1:T(8,128)(2,1)} %bitcast.7) | data formatting | bytes 458752
  93.0 1.7 %copy.15 = bf16[256,576]{0,1:T(8,128)(2,1)} copy(bf16[256,576]{0,1:T(8,128)(2,1)} %bitcast.6) | data formatting | bytes 589824

commit v3 on v2

--- a/solution.py
+++ b/solution.py
@@ -43,7 +43,7 @@
     part, part_recv, ysum, yrecv, zsend, zrecv,
     cos_ref, sin_ref, queries, cache, m_ref, l_ref, acc,
     hv, hv_recv, far_send, far_recv, near_send, near_recv, zo_send, zo_recv, fin, fin_recv,
-    ld_sem, wo_ssem, wo_rsem, p_sem, y_sem, z_sem, p1_sem, p2_sem, p3_sem, p4_sem, sh_sem,
+    ld_sem, wo_ssem, wo_rsem, p_sem, y_sem, z_sem, p1_sem, p2_sem, p3_sem, sh_sem,
     hv_sem, far_sem, near_sem, zo_sem, fin_sem,
 ):
     c_idx = lax.axis_index("ctx")
@@ -169,34 +169,22 @@
     def half(b, c, e):
         return cache.at[pl.ds(at(k, b, c, 0, 64 * e), 64)]
 
-    c_up, c_down = device(dy=j, dx=k), device(dy=-j, dx=-k)
+    c_peers = (device(dy=j, dx=k), device(dy=-j, dx=-k), device(dy=2 * j, dx=2 * k))
     mine = group(zl, c_own)
-    mine_half = half(zl, c_own, 0)
 
     def share(r, i, src):
         remote(src, src, sh_sem.at[r, i], sibling).start()
 
     def send_group(r, b):
         src = group(b, c_own)
-        remote(src, src, p3_sem.at[r, 0], c_up).start()
-        remote(src, src, p3_sem.at[r, 1], c_down).start()
+        for i, peer in enumerate(c_peers):
+            remote(src, src, p3_sem.at[r, i], peer).start()
         share(r, 3, src)
 
-    def near_groups(r, b):
-        below, above = (c_own + 3) % 4, (c_own + 1) % 4
-        remote(mine, mine, p3_sem.at[r, 0], sibling).wait_recv()
-        src = half(b, below, 0)
-        remote(src, src, p4_sem.at[r, 0], c_up).start()
-        share(r, 0, group(b, below))
-        remote(mine, mine, p3_sem.at[r, 1], sibling).wait_recv()
-        src = half(b, above, 1)
-        remote(src, src, p4_sem.at[r, 1], c_down).start()
-        share(r, 1, group(b, above))
-
-    def far_group(r, b):
-        for e in range(2):
-            remote(mine_half, mine_half, p4_sem.at[r, e], sibling).wait_recv()
-        share(r, 2, group(b, (c_own + 2) % 4))
+    def receive(r, b):
+        for i, d in enumerate((1, -1, 2)):
+            remote(mine, mine, p3_sem.at[r, i], sibling).wait_recv()
+            share(r, i, group(b, (c_own - d + 4) % 4))
 
     def shared(r):
         for i in range(4):
@@ -262,8 +250,7 @@
     send_group(1, place_of(1))
     second_phase[1].wait()
     send_group(2, place_of(2))
-    near_groups(0, zl)
-    far_group(0, zl)
+    receive(0, zl)
     attend(k, zl)
     second_phase[2].wait()
     second_phase[3].wait()
@@ -271,10 +258,9 @@
 
     def round_of(r, b_last):
         b = place_of(r)
-        near_groups(r, b)
         shared(r - 1)
         attend(j, b_last)
-        far_group(r, b)
+        receive(r, b)
         attend(k, b)
         return b
 
@@ -413,9 +399,8 @@
     theirs = jnp.where(k == 0, theirs[:, :448], theirs[:, 448:])
     out_ref[:, pl.ds(pl.multiple_of(j * HALF, HALF), HALF)] = theirs.T
     for r in range(4):
-        for i in range(2):
+        for i in range(3):
             remote(mine, mine, p3_sem.at[r, i], sibling).wait_send()
-            remote(mine_half, mine_half, p4_sem.at[r, i], sibling).wait_send()
         for i in range(4):
             remote(mine, mine, sh_sem.at[r, i], sibling).wait_send()
 
@@ -448,7 +433,7 @@
             V((2, 2, 2, 64, BLK), BF16), V((2, 2, 2, 64, BLK), BF16),
             V((HALF, BLK), BF16), V((HALF, BLK), BF16), V((HALF, BLK), BF16), V((HALF, BLK), BF16),
             dma((7,)), dma, dma, dma((2,)), dma((3, 2)), dma((2,)), dma((3, 2)), dma((4, 2)),
-            dma((4, 2, 2)), dma((4, 2, 2)), dma((4, 4, 2)), dma((2,)), dma((5, 2, 2)), dma((5, 2, 2, 2)),
+            dma((4, 3, 2)), dma((4, 4, 2)), dma((2,)), dma((5, 2, 2)), dma((5, 2, 2, 2)),
             dma((3, 2)), dma((2, 2)),
         ],
         compiler_params=pltpu.CompilerParams(

time: 94.9 us -> 83.1 us (0.88)
  Pallas kernels: 90.7 us -> 78.9 us
    pallas_call x1, Pallas kernels: 90.7 us -> 78.9 us  [per_device(): pl.pallas_call(kernel, out_shape=(jax.ShapeDtypeStruct((448, ROWS), BF16)...]
where the time goes in v3:
time: 83.1 us; the launch traced here: 82.9 us
  Pallas kernels  78.9 us (95%)
  local copies, waits for them, and re-layouts  3.33 us (4%)
    pallas_call x1, Pallas kernels, per_device(): pl.pallas_call(kernel, out_shape=(jax.ShapeDtypeStruct((448, ROWS), BF16)...  78.9 us
    unnamed x2, local copies, waits for them, and re-layouts  3.33 us

profile of v3, /device:TPU:1, one launch (start us, length us, event | category | flops | bytes accessed | tf_op | source)
XLA Modules:
  0.0 82.9 jit_solution(5611786235750782767)
XLA Ops:
  0.6 78.9 %shard_map.113 = (bf16[448,256]{1,0:T(8,128)(2,1)}, bf16[576,256]{1,0:T(8,128)(2,1)}) custom-call(bf16[448,256]{1,0:T(8,128)(2,1)} %bitcast.8, bf16[256,1536]{1,0:T(8,128)(2,1)} %ql_hbm.1, bf16[448,576]{1,0:T(8,128)(2,1)} %wdkv_hbm.1, f32[1,512]{1,0:T(1,128)} %bitcast.10, bf16[1536,768]{1,0:T(8,128)(2,1)} %wuq_hbm.1, bf16[4,512,128]{2,1,0:T(8,128)(2,1)} %wuk_hbm.1, ...), custom_call_target="tpu_custom_call" | custom-call | tf_op jit(solution)/shard_map/pallas_call | solution.py:416
  79.6 1.6 %copy.14 = bf16[256,448]{0,1:T(8,128)(2,1)} copy(bf16[256,448]{0,1:T(8,128)(2,1)} %bitcast.7) | data formatting | bytes 458752
  81.2 1.7 %copy.15 = bf16[256,576]{0,1:T(8,128)(2,1)} copy(bf16[256,576]{0,1:T(8,128)(2,1)} %bitcast.6) | data formatting | bytes 589824

commit v4 on v3

--- a/solution.py
+++ b/solution.py
@@ -42,9 +42,9 @@
     li, ql, wdkv, wuq, wuk, wuv, wo, wo2,
     part, part_recv, ysum, yrecv, zsend, zrecv,
     cos_ref, sin_ref, queries, cache, m_ref, l_ref, acc,
-    hv, hv_recv, far_send, far_recv, near_send, near_recv, zo_send, zo_recv, fin, fin_recv,
+    hv, hv_recv, far_send, far_recv, near_send, near_recv, direct_send, direct_recv, zo_send, zo_recv, fin, fin_recv,
     ld_sem, wo_ssem, wo_rsem, p_sem, y_sem, z_sem, p1_sem, p2_sem, p3_sem, sh_sem,
-    hv_sem, far_sem, near_sem, zo_sem, fin_sem,
+    hv_sem, far_sem, near_sem, direct_sem, zo_sem, fin_sem,
 ):
     c_idx = lax.axis_index("ctx")
     t_idx = lax.axis_index("tp")
@@ -269,35 +269,21 @@
     attend(j, b_last)
 
     loads[5].wait()
-    for h in range(HEADS):
-        context = (acc[h] / l_ref[h][:, :1]).astype(BF16)
-        hv[:, 128 * h : 128 * (h + 1)] = dot(context, wuv[h]).astype(BF16)
-    hv_copy = remote(hv.at[pl.ds(pl.multiple_of(j * HALF, HALF), HALF)], hv_recv, hv_sem, sibling)
+
+    def head_values(rows):
+        for h in range(HEADS):
+            context = (acc[h, rows, :] / l_ref[h, rows, :1]).astype(BF16)
+            hv[rows, 128 * h : 128 * (h + 1)] = dot(context, wuv[h]).astype(BF16)
+
+    hv_own_rows = pl.ds(pl.multiple_of(k * HALF, HALF), HALF)
+    hv_sibling_rows = pl.ds(pl.multiple_of(j * HALF, HALF), HALF)
+    head_values(hv_sibling_rows)
+    hv_copy = remote(hv.at[hv_sibling_rows], hv_recv, hv_sem, sibling)
     hv_copy.start()
-
-    number = lax.broadcasted_iota(jnp.int32, (1, 32), 1)
-    sources = []
-    for i in range(2):
-        prompt = jnp.sum(jnp.where(slot_row[...] == 2 * c_idx + i, number, 0), axis=1, keepdims=True)
-        held = jnp.sum(jnp.where(order_row[...] == prompt, number, 0), axis=1, keepdims=True)
-        core, hx, hz = held & 1, held >> 3, (held >> 1) & 3
-        row = row_id[:HALF]
-        q, rest = row >> 5, row & 31
-        zero = hz * 512 + q * 128 + hx * 32 + rest
-        one = 2048 + hz * 512 + hx * 128 + q * 32 + rest
-        sources.append(jnp.where(core == 0, zero, one))
-    source = jnp.concatenate(sources, 0)
-    key_lane = lax.broadcasted_iota(jnp.int32, (1, 1024), 1)
-    picked_rows = jnp.zeros((ROWS, KVW), F32)
-    for n in range(4):
-        picked = jnp.where(key_lane + 1024 * n == source, 1.0, 0.0).astype(BF16)
-        picked_rows = picked_rows + dot(picked, cache[1024 * n : 1024 * (n + 1), :])
-    own_ref[...] = picked_rows.T.astype(BF16)
-
+    head_values(hv_own_rows)
     loads[6].wait()
     wo_far.wait()
     hv_copy.wait()
-    hv_own_rows = pl.ds(pl.multiple_of(k * HALF, HALF), HALF)
 
     up, down = device(dy=1), device(dy=-1)
     chunks = ((0, 0, 256), (0, 256, 256), (0, 512, 384), (1, 0, 512), (1, 512, 384))
@@ -322,6 +308,16 @@
 
     def near_copy(n, e, f, where):
         return remote(span(near_send.at[e, f], n), span(near_recv.at[e, f], n), near_sem.at[n, e, f], where)
+
+    direct_peers = ((1, up), (-1, down), (2, device(dy=2)))
+
+    def direct_copy(i, where):
+        return remote(direct_send.at[i], direct_recv.at[i], direct_sem.at[i], where)
+
+    def direct_out():
+        for i, (dy, where) in enumerate(direct_peers):
+            direct_send[i] = partial(dy, 0).astype(BF16)
+            direct_copy(i, where).start()
 
     held = {}
 
@@ -346,15 +342,20 @@
     def finish(n):
         s, first_column, width = chunks[n]
         columns = pl.ds(first_column, width)
-        p = partial(0, n)
-        for e, where in enumerate((up, down)):
-            for f in range(2):
-                near_copy(n, e, f, where).wait()
-        sums = [
-            span(near_recv.at[0, f], n)[...].astype(F32) + span(near_recv.at[1, f], n)[...].astype(F32)
-            for f in range(2)
-        ]
-        total = p + jnp.concatenate(sums, 0)
+        total = partial(0, n)
+        if n == 0:
+            for i, (_, where) in enumerate(direct_peers):
+                direct_copy(i, where).wait()
+                total = total + direct_recv[i].astype(F32)
+        else:
+            for e, where in enumerate((up, down)):
+                for f in range(2):
+                    near_copy(n, e, f, where).wait()
+            sums = [
+                span(near_recv.at[0, f], n)[...].astype(F32) + span(near_recv.at[1, f], n)[...].astype(F32)
+                for f in range(2)
+            ]
+            total = total + jnp.concatenate(sums, 0)
         if s == 0:
             zo_send[:, columns] = total.astype(BF16)
             cp = remote(zo_send.at[:, columns], zo_recv.at[:, columns], zo_sem.at[n], device(dz=4))
@@ -370,34 +371,49 @@
         columns = pl.ds(chunks[n][1], chunks[n][2])
         return remote(fin.at[:, columns], fin_recv.at[:, columns], fin_sem.at[n - 3], sibling)
 
-    far_out(0)
-    near_out(0)
+    def pick_owned():
+        number = lax.broadcasted_iota(jnp.int32, (1, 32), 1)
+        sources = []
+        for i in range(2):
+            prompt = jnp.sum(jnp.where(slot_row[...] == 2 * c_idx + i, number, 0), axis=1, keepdims=True)
+            held = jnp.sum(jnp.where(order_row[...] == prompt, number, 0), axis=1, keepdims=True)
+            core, hx, hz = held & 1, held >> 3, (held >> 1) & 3
+            row = row_id[:HALF]
+            q, rest = row >> 5, row & 31
+            zero = hz * 512 + q * 128 + hx * 32 + rest
+            one = 2048 + hz * 512 + hx * 128 + q * 32 + rest
+            sources.append(jnp.where(core == 0, zero, one))
+        source = jnp.concatenate(sources, 0)
+        key_lane = lax.broadcasted_iota(jnp.int32, (1, 1024), 1)
+        picked_rows = jnp.zeros((ROWS, KVW), F32)
+        for n in range(4):
+            picked = jnp.where(key_lane + 1024 * n == source, 1.0, 0.0).astype(BF16)
+            picked_rows = picked_rows + dot(picked, cache[1024 * n : 1024 * (n + 1), :])
+        own_ref[...] = picked_rows.T.astype(BF16)
+
     far_out(1)
-    near_added(0)
+    direct_out()
     near_out(1)
     far_out(2)
+    near_out(2)
     near_added(1)
-    near_out(2)
     finish(0)
+    near_added(2)
     far_out(3)
-    near_added(2)
     near_out(3)
     finish(1)
     far_out(4)
+    near_out(4)
     near_added(3)
-    near_out(4)
+    pick_owned()
     finish(2)
     near_added(4)
     finish(3)
     finish(4)
-    mine_here = fin[...]
-    mine_here = jnp.where(k == 0, mine_here[:, :448], mine_here[:, 448:])
-    out_ref[:, hv_own_rows] = mine_here.T
+    out_ref[hv_own_rows, :] = fin[...]
     fin_copy(3).wait()
     fin_copy(4).wait()
-    theirs = fin_recv[...]
-    theirs = jnp.where(k == 0, theirs[:, :448], theirs[:, 448:])
-    out_ref[:, pl.ds(pl.multiple_of(j * HALF, HALF), HALF)] = theirs.T
+    out_ref[hv_sibling_rows, :] = fin_recv[...]
     for r in range(4):
         for i in range(3):
             remote(mine, mine, p3_sem.at[r, i], sibling).wait_send()
@@ -416,7 +432,7 @@
     out, own = pl.pallas_call(
         kernel,
         out_shape=(
-            jax.ShapeDtypeStruct((448, ROWS), BF16),
+            jax.ShapeDtypeStruct((ROWS, BLK), BF16),
             jax.ShapeDtypeStruct((KVW, ROWS), BF16),
         ),
         in_specs=[hbm, hbm, hbm, vmem, hbm, hbm, hbm, hbm, smem, vmem, vmem],
@@ -431,9 +447,11 @@
             V((ROWS, 512), BF16), V((HALF, 512), BF16),
             V((2, 2, 64, BLK), BF16), V((2, 2, 64, BLK), BF16),
             V((2, 2, 2, 64, BLK), BF16), V((2, 2, 2, 64, BLK), BF16),
+            V((3, HALF, 256), BF16), V((3, HALF, 256), BF16),
             V((HALF, BLK), BF16), V((HALF, BLK), BF16), V((HALF, BLK), BF16), V((HALF, BLK), BF16),
             dma((7,)), dma, dma, dma((2,)), dma((3, 2)), dma((2,)), dma((3, 2)), dma((4, 2)),
             dma((4, 3, 2)), dma((4, 4, 2)), dma((2,)), dma((5, 2, 2)), dma((5, 2, 2, 2)),
+            dma((3, 2)),
             dma((3, 2)), dma((2, 2)),
         ],
         compiler_params=pltpu.CompilerParams(
@@ -443,6 +461,22 @@
         layer_input.T, q_latent, w_dkv, kv_gain.reshape(1, LAT), w_uq, w_uk, w_uv, w_o,
         block_order, block_order.reshape(1, 32), owner_slot.reshape(1, 32),
     )
+
+    def hand_over(block, owned, out_ref, own_ref):
+        core = lax.axis_index("tp") % 2
+        block = block[...]
+        out_ref[...] = jnp.where(core == 0, block[:, :448], block[:, 448:]).T
+        own_ref[...] = owned[...]
+
+    out, own = pl.pallas_call(
+        hand_over,
+        out_shape=(
+            jax.ShapeDtypeStruct((448, ROWS), BF16),
+            jax.ShapeDtypeStruct((KVW, ROWS), BF16),
+        ),
+        in_specs=[vmem, vmem],
+        out_specs=(vmem, vmem),
+    )(out, own)
     return out.T, own.T
 
 

time: 83.1 us -> 82 us (0.987)
  local copies, waits for them, and re-layouts: 3.33 us -> 0 us
  Pallas kernels: 78.9 us -> 81.2 us
    unnamed x2 -> x0, local copies, waits for them, and re-layouts: 3.33 us -> none
    pallas_call x1 -> x2, Pallas kernels: 78.9 us -> 81.2 us  [the longest x1 79.1 us: per_device(): pl.pallas_call(kernel, out_shape=(jax.ShapeDtypeStruct((ROWS, BLK), BF16)...]
where the time goes in v4:
time: 82 us; the launch traced here: 81.9 us
  Pallas kernels  81.2 us (99%)
    pallas_call x1, Pallas kernels, per_device(): pl.pallas_call(kernel, out_shape=(jax.ShapeDtypeStruct((ROWS, BLK), BF16)...  79.1 us
    pallas_call x1, Pallas kernels, per_device(): pl.pallas_call(hand_over, out_shape=(jax.ShapeDtypeStruct((448, ROWS), BF...  2.07 us

profile of v4, /device:TPU:1, one launch (start us, length us, event | category | flops | bytes accessed | tf_op | source)
XLA Modules:
  0.0 81.9 jit_solution(4380428346149113857)
XLA Ops:
  0.6 79.1 %shard_map.113 = (bf16[256,896]{1,0:T(8,128)(2,1)}, bf16[576,256]{1,0:T(8,128)(2,1)}) custom-call(bf16[448,256]{1,0:T(8,128)(2,1)} %bitcast.6, bf16[256,1536]{1,0:T(8,128)(2,1)} %ql_hbm.1, bf16[448,576]{1,0:T(8,128)(2,1)} %wdkv_hbm.1, f32[1,512]{1,0:T(1,128)} %bitcast.8, bf16[1536,768]{1,0:T(8,128)(2,1)} %wuq_hbm.1, bf16[4,512,128]{2,1,0:T(8,128)(2,1)} %wuk_hbm.1, ...), custom_call_target="tpu_custom_call" | custom-call | tf_op jit(solution)/shard_map/pallas_call | solution.py:432
  79.8 2.1 %shard_map.114 = (bf16[448,256]{1,0:T(8,128)(2,1)}, bf16[576,256]{1,0:T(8,128)(2,1)}) custom-call(bf16[256,896]{1,0:T(8,128)(2,1)} %get-tuple-element.6.block, bf16[576,256]{1,0:T(8,128)(2,1)} %get-tuple-element.7.owned), custom_call_target="tpu_custom_call" | custom-call | tf_op jit(solution)/shard_map/pallas_call | solution.py:471

commit v5 on v4

--- a/solution.py
+++ b/solution.py
@@ -78,7 +78,7 @@
     peers = [
         sibling, device(dy=1), device(dy=-1), device(dy=2), device(dz=4),
         device(dx=1), device(dx=-1), device(dx=2),
-        device(dz=1), device(dz=-1), device(dz=2), device(dz=-2),
+        device(dz=1), device(dz=-1),
     ]
     for peer in peers:
         pl.semaphore_signal(barrier, inc=1, device_id=peer, device_id_type=MESH)
@@ -191,8 +191,8 @@
             remote(mine, mine, sh_sem.at[r, i], sibling).wait_recv()
 
     second_phase = []
-    for i, (src, d) in enumerate(((mine, 1), (mine, -1), (half(zl, c_own, 0), 2), (half(zl, c_own, 1), -2))):
-        cp = remote(src, src, p2_sem.at[i], device(dz=d))
+    for i, d in enumerate((1, -1)):
+        cp = remote(mine, mine, p2_sem.at[i], device(dz=d))
         cp.start()
         second_phase.append(cp)
 
@@ -246,10 +246,14 @@
         return (zl + 3 - 2 * (r - 1) + 3 * ((r - 1) * (r - 2) // 2)) % 4
 
     send_group(0, zl)
-    second_phase[0].wait()
-    send_group(1, place_of(1))
-    second_phase[1].wait()
-    send_group(2, place_of(2))
+    for i, d in enumerate((1, -1)):
+        b = place_of(i + 1)
+        second_phase[i].wait()
+        forwarded = half(b, c_own, i)
+        cp = remote(forwarded, forwarded, p2_sem.at[i + 2], device(dz=d))
+        cp.start()
+        second_phase.append(cp)
+        send_group(i + 1, b)
     receive(0, zl)
     attend(k, zl)
     second_phase[2].wait()
@@ -400,14 +404,14 @@
     finish(0)
     near_added(2)
     far_out(3)
+    far_out(4)
     near_out(3)
     finish(1)
-    far_out(4)
     near_out(4)
     near_added(3)
-    pick_owned()
     finish(2)
     near_added(4)
+    pick_owned()
     finish(3)
     finish(4)
     out_ref[hv_own_rows, :] = fin[...]

time: 82 us -> 79.8 us (0.973)
  Pallas kernels: 81.2 us -> 79 us
    pallas_call x1, Pallas kernels: 79.1 us -> 76.9 us  [per_device(): pl.pallas_call(kernel, out_shape=(jax.ShapeDtypeStruct((ROWS, BLK), BF16)...]
where the time goes in v5:
time: 79.8 us; the launch traced here: 79.6 us
  Pallas kernels  79 us (99%)
    pallas_call x1, Pallas kernels, per_device(): pl.pallas_call(kernel, out_shape=(jax.ShapeDtypeStruct((ROWS, BLK), BF16)...  76.9 us
    pallas_call x1, Pallas kernels, per_device(): pl.pallas_call(hand_over, out_shape=(jax.ShapeDtypeStruct((448, ROWS), BF...  2.07 us

profile of v5, /device:TPU:1, one launch (start us, length us, event | category | flops | bytes accessed | tf_op | source)
XLA Modules:
  0.0 79.6 jit_solution(9617300263589509377)
XLA Ops:
  0.6 76.9 %shard_map.113 = (bf16[256,896]{1,0:T(8,128)(2,1)}, bf16[576,256]{1,0:T(8,128)(2,1)}) custom-call(bf16[448,256]{1,0:T(8,128)(2,1)} %bitcast.6, bf16[256,1536]{1,0:T(8,128)(2,1)} %ql_hbm.1, bf16[448,576]{1,0:T(8,128)(2,1)} %wdkv_hbm.1, f32[1,512]{1,0:T(1,128)} %bitcast.8, bf16[1536,768]{1,0:T(8,128)(2,1)} %wuq_hbm.1, bf16[4,512,128]{2,1,0:T(8,128)(2,1)} %wuk_hbm.1, ...), custom_call_target="tpu_custom_call" | custom-call | tf_op jit(solution)/shard_map/pallas_call | solution.py:436
  77.6 2.1 %shard_map.114 = (bf16[448,256]{1,0:T(8,128)(2,1)}, bf16[576,256]{1,0:T(8,128)(2,1)}) custom-call(bf16[256,896]{1,0:T(8,128)(2,1)} %get-tuple-element.6.block, bf16[576,256]{1,0:T(8,128)(2,1)} %get-tuple-element.7.owned), custom_call_target="tpu_custom_call" | custom-call | tf_op jit(solution)/shard_map/pallas_call | solution.py:475

commit v6 on v5

--- a/solution.py
+++ b/solution.py
@@ -38,12 +38,12 @@
 
 def kernel(
     li_hbm, ql_hbm, wdkv_hbm, gain_ref, wuq_hbm, wuk_hbm, wuv_hbm, wo_hbm, order_ref, order_row, slot_row,
-    out_ref, own_ref,
+    out_hbm, own_hbm,
     li, ql, wdkv, wuq, wuk, wuv, wo, wo2,
     part, part_recv, ysum, yrecv, zsend, zrecv,
     cos_ref, sin_ref, queries, cache, m_ref, l_ref, acc,
     hv, hv_recv, far_send, far_recv, near_send, near_recv, direct_send, direct_recv, zo_send, zo_recv, fin, fin_recv,
-    ld_sem, wo_ssem, wo_rsem, p_sem, y_sem, z_sem, p1_sem, p2_sem, p3_sem, sh_sem,
+    out_ref, own_ref, out_sem, ld_sem, wo_ssem, wo_rsem, p_sem, y_sem, z_sem, p1_sem, p2_sem, p3_sem, sh_sem,
     hv_sem, far_sem, near_sem, direct_sem, zo_sem, fin_sem,
 ):
     c_idx = lax.axis_index("ctx")
@@ -394,6 +394,7 @@
             picked = jnp.where(key_lane + 1024 * n == source, 1.0, 0.0).astype(BF16)
             picked_rows = picked_rows + dot(picked, cache[1024 * n : 1024 * (n + 1), :])
         own_ref[...] = picked_rows.T.astype(BF16)
+        pltpu.make_async_copy(own_ref, own_hbm, out_sem.at[0]).start()
 
     far_out(1)
     direct_out()
@@ -414,15 +415,18 @@
     pick_owned()
     finish(3)
     finish(4)
-    out_ref[hv_own_rows, :] = fin[...]
+    pltpu.make_async_copy(fin, out_hbm.at[hv_own_rows], out_sem.at[1]).start()
     fin_copy(3).wait()
     fin_copy(4).wait()
-    out_ref[hv_sibling_rows, :] = fin_recv[...]
+    pltpu.make_async_copy(fin_recv, out_hbm.at[hv_sibling_rows], out_sem.at[2]).start()
     for r in range(4):
         for i in range(3):
             remote(mine, mine, p3_sem.at[r, i], sibling).wait_send()
         for i in range(4):
             remote(mine, mine, sh_sem.at[r, i], sibling).wait_send()
+    pltpu.make_async_copy(own_ref, own_hbm, out_sem.at[0]).wait()
+    pltpu.make_async_copy(fin, out_hbm.at[hv_own_rows], out_sem.at[1]).wait()
+    pltpu.make_async_copy(fin_recv, out_hbm.at[hv_sibling_rows], out_sem.at[2]).wait()
 
 
 def per_device(
@@ -440,7 +444,7 @@
             jax.ShapeDtypeStruct((KVW, ROWS), BF16),
         ),
         in_specs=[hbm, hbm, hbm, vmem, hbm, hbm, hbm, hbm, smem, vmem, vmem],
-        out_specs=(vmem, vmem),
+        out_specs=(hbm, hbm),
         scratch_shapes=[
             V((448, ROWS), BF16), V((ROWS, 1536), BF16), V((448, KVW), BF16), V((1536, 768), BF16),
             V((HEADS, LAT, NOPE), BF16), V((HEADS, LAT, NOPE), BF16), V((512, MODEL), BF16), V((512, MODEL), BF16),
@@ -453,7 +457,7 @@
             V((2, 2, 2, 64, BLK), BF16), V((2, 2, 2, 64, BLK), BF16),
             V((3, HALF, 256), BF16), V((3, HALF, 256), BF16),
             V((HALF, BLK), BF16), V((HALF, BLK), BF16), V((HALF, BLK), BF16), V((HALF, BLK), BF16),
-            dma((7,)), dma, dma, dma((2,)), dma((3, 2)), dma((2,)), dma((3, 2)), dma((4, 2)),
+            V((ROWS, BLK), BF16), V((KVW, ROWS), BF16), dma((3,)), dma((7,)), dma, dma, dma((2,)), dma((3, 2)), dma((2,)), dma((3, 2)), dma((4, 2)),
             dma((4, 3, 2)), dma((4, 4, 2)), dma((2,)), dma((5, 2, 2)), dma((5, 2, 2, 2)),
             dma((3, 2)),
             dma((3, 2)), dma((2, 2)),

time: 79.8 us -> 79.5 us (level)
  no operation moved by 1% of the time
where the time goes in v6:
time: 79.5 us; the launch traced here: 79.4 us
  Pallas kernels  78.7 us (99%)
    pallas_call x1, Pallas kernels, per_device(): pl.pallas_call(kernel, out_shape=(jax.ShapeDtypeStruct((ROWS, BLK), BF16)...  76.7 us
    pallas_call x1, Pallas kernels, per_device(): pl.pallas_call(hand_over, out_shape=(jax.ShapeDtypeStruct((448, ROWS), BF...  2.07 us

profile of v6, /device:TPU:1, one launch (start us, length us, event | category | flops | bytes accessed | tf_op | source)
XLA Modules:
  0.0 79.4 jit_solution(6997451775637590905)
XLA Ops:
  0.6 76.7 %shard_map.113 = (bf16[256,896]{1,0:T(8,128)(2,1)}, bf16[576,256]{1,0:T(8,128)(2,1)}) custom-call(bf16[448,256]{1,0:T(8,128)(2,1)} %bitcast.6, bf16[256,1536]{1,0:T(8,128)(2,1)} %ql_hbm.1, bf16[448,576]{1,0:T(8,128)(2,1)} %wdkv_hbm.1, f32[1,512]{1,0:T(1,128)} %bitcast.8, bf16[1536,768]{1,0:T(8,128)(2,1)} %wuq_hbm.1, bf16[4,512,128]{2,1,0:T(8,128)(2,1)} %wuk_hbm.1, ...), custom_call_target="tpu_custom_call" | custom-call | tf_op jit(solution)/shard_map/pallas_call | solution.py:440
  77.3 2.1 %shard_map.114 = (bf16[448,256]{1,0:T(8,128)(2,1)}, bf16[576,256]{1,0:T(8,128)(2,1)}) custom-call(bf16[256,896]{1,0:T(8,128)(2,1)} %get-tuple-element.6.block, bf16[576,256]{1,0:T(8,128)(2,1)} %get-tuple-element.7.owned), custom_call_target="tpu_custom_call" | custom-call | tf_op jit(solution)/shard_map/pallas_call | solution.py:479
